TPU v7x, 256 devices: a whole 4x4x8 slice. The times are simulated.
256 devices in a mesh: ctx: 16 (over y, x), exp: 8 (over z), half: 2 (over core).
Axes of the slice: x: 4, y: 4, z: 8, core: 2. Of those that a mesh axis runs over, the one named last changes fastest.
Arguments:
- residual: bfloat16 [2048, 4096], P(('ctx', 'exp', 'half')), may hold values from -6 to 6
- mixer_input: bfloat16 [2048, 8192], P('ctx', ('exp', 'half')), may hold values from -6 to 6
- mixer_gate: bfloat16 [2048, 8192], P('ctx', ('exp', 'half')), may hold values from -6 to 6
- step_size: float32 [2048, 8192], P('ctx', ('exp', 'half')), may hold values from 0 to 2, as said below
- decay_rate: float32 [16, 8192], P(None, ('exp', 'half')), may hold values from 0.02 to 8
- state_in: float32 [2048, 16], P('ctx'), may hold values from -6 to 6
- state_out: float32 [2048, 16], P('ctx'), may hold values from -6 to 6
- skip_weight: float32 [8192], P(('exp', 'half')), may hold values from 0.5 to 1.5
- projection: bfloat16 [8192, 4096], P(('exp', 'half')), may hold values from -0.0625 to 0.0625
- norm_gain: float32 [4096], replicated, may hold values from 0.1 to 1.9
- routes: int32 [2048, 2], P('ctx'), may hold values from 0 to 7, all different within a row; in each aligned block of 128 rows (0 to 127, 128 to 255, ...) at most 64 rows name the same one
- route_weight: float32 [2048, 2], P('ctx'), may hold values from 0.2 to 1
- up_weight: bfloat16 [8, 4096, 12288], P('exp', None, ('ctx', 'half')), may hold values from -0.09375 to 0.09375
- down_weight: bfloat16 [8, 12288, 4096], P('exp', ('ctx', 'half')), may hold values from -0.0546875 to 0.0546875
Outputs:
- mixed: bfloat16 [2048, 4096], P(('ctx', 'exp', 'half'))
Inputs may be any that keep to these rules, and one draw needn't show every extreme that they name: `routes`: the two experts of a token differ. Within each block of 128 consecutive positions every expert is named by at most 64 tokens, and in some block one expert is named by exactly 64. `step_size`: Positive.
All inputs are finite; a program needn't handle non-finite values.
Results may differ from a plain program's by a relative error of at most 0.0075.
Values may be sent and summed in bfloat16 or wider, within the bound.
A program may use at most 128 MiB of HBM per device.

v0:
```python
import functools

import jax
import jax.numpy as jnp
from jax import lax
from jax.experimental import pallas as pl
from jax.experimental.pallas import tpu as pltpu
from jax.sharding import PartitionSpec as P

F32 = jnp.float32
BF16 = jnp.bfloat16
TOK = 128
CH = 512
NS = 16
D = 4096
HD = 2048
FFL = 384
NZ = 8
NCTX = 16


def layer_kernel(
    residual,
    xin,
    gate,
    step,
    rate,
    sin,
    sout,
    skip,
    proj_hbm,
    gain,
    routes,
    rweight,
    up_hbm,
    down_hbm,
    out,
    proj,
    up,
    down,
    dec,
    drive,
    yacc,
    trans,
    carry,
    gsend,
    gmine,
    gpeer,
    psend,
    precv,
    own16,
    upd16,
    rows,
    chooser,
    selsend,
    selpeer,
    x,
    hid,
    part,
    r1,
    r2,
    r3,
    r4,
    qsend,
    q0,
    outs,
    csend,
    crecv,
    wsem,
    wsend,
    wrecv,
    carry_s,
    carry_r,
    one_s,
    one_r,
    zs1,
    zr1,
    zs2,
    zr2,
    zs3,
    zr3,
    ag_s,
    ag_r,
    s1,
    r1s,
    s2,
    r2s,
    s3,
    r3s,
    s4,
    r4s,
):
    c = lax.axis_index("ctx")
    z = lax.axis_index("exp")
    h = lax.axis_index("half")
    sending = []

    def send(src, dst, ssem, rsem, to):
        copy = pltpu.make_async_remote_copy(
            src_ref=src,
            dst_ref=dst,
            send_sem=ssem,
            recv_sem=rsem,
            device_id=to,
            device_id_type=pl.DeviceIdType.MESH,
        )
        copy.start()
        sending.append(copy)

    def arrived(dst, ssem, rsem):
        pltpu.make_async_remote_copy(
            src_ref=dst,
            dst_ref=dst,
            send_sem=ssem,
            recv_sem=rsem,
            device_id=sibling,
            device_id_type=pl.DeviceIdType.MESH,
        ).wait_recv()

    sibling = {"ctx": c, "exp": z, "half": 1 - h}

    def zpeer(d):
        return {"ctx": c, "exp": lax.rem(z + d, NZ), "half": h}

    cy, cx = lax.div(c, 4), lax.rem(c, 4)
    a = cx + h * (cy - cx)
    b = cy + h * (cx - cy)

    def ctx_at(da, db):
        return lax.rem(a + da, 4) * (1 + 3 * h) + lax.rem(b + db, 4) * (4 - 3 * h)

    def apeer(d):
        return {"ctx": ctx_at(d, 0), "exp": z, "half": h}

    def bpeer(d):
        return {"ctx": ctx_at(0, d), "exp": z, "half": h}

    local = [
        pltpu.make_async_copy(proj_hbm, proj.at[pl.ds(0, CH)], wsem.at[0]),
        pltpu.make_async_copy(up_hbm.at[0], up.at[:, pl.ds(0, FFL)], wsem.at[1]),
        pltpu.make_async_copy(down_hbm.at[0], down.at[pl.ds(0, FFL)], wsem.at[2]),
    ]
    for copy in local:
        copy.start()

    barrier = pltpu.get_barrier_semaphore()
    for d in range(1, NCTX):
        pl.semaphore_signal(
            barrier,
            inc=1,
            device_id={"ctx": lax.rem(c + d, NCTX), "exp": z, "half": h},
            device_id_type=pl.DeviceIdType.MESH,
        )
    for d in range(1, NZ):
        pl.semaphore_signal(
            barrier, inc=1, device_id=zpeer(d), device_id_type=pl.DeviceIdType.MESH
        )
    pl.semaphore_signal(
        barrier, inc=1, device_id=sibling, device_id_type=pl.DeviceIdType.MESH
    )
    pl.semaphore_wait(barrier, NCTX - 1 + NZ - 1 + 1)

    send(proj_hbm, proj.at[pl.ds(CH, CH)], wsend.at[0], wrecv.at[0], sibling)

    nrate = -rate[...]
    trans[...] = jnp.zeros_like(trans)
    trans[:, 0:NS] = sin[...]
    trans[:, NS : 2 * NS] = sout[...]
    trans[...] = trans[...].T
    drive[...] = step[...] * xin[...].astype(F32)

    def turned(first, base):
        return pltpu.roll(trans[first : first + NS, :], lax.rem(TOK - base, TOK), 1)

    def first_pass(tb, state):
        base = pl.multiple_of(tb * 8, 8)
        st8 = step[pl.ds(base, 8), :]
        dr8 = drive[pl.ds(base, 8), :]
        ins = turned(0, base)
        for i in range(8):
            decay = jnp.exp(st8[i : i + 1, :] * nrate)
            dec[base + i] = decay
            state = decay * state + dr8[i : i + 1, :] * ins[:, i : i + 1]
        return state

    zero_state = jnp.zeros((NS, CH), F32)
    carry[c, 0:NS, :] = lax.fori_loop(0, TOK // 8, first_pass, zero_state)
    carry[c, NS : NS + 8, :] = jnp.broadcast_to(
        jnp.sum(step[...], axis=0, keepdims=True), (8, CH)
    )

    for d in range(1, NCTX):

        @pl.when(c + d < NCTX)
        def _():
            pltpu.make_async_remote_copy(
                src_ref=carry.at[c],
                dst_ref=carry.at[c],
                send_sem=carry_s.at[d],
                recv_sem=carry_r.at[d],
                device_id={"ctx": c + d, "exp": z, "half": h},
                device_id_type=pl.DeviceIdType.MESH,
            ).start()

    send(up_hbm.at[0], up.at[:, pl.ds(FFL, FFL)], wsend.at[1], wrecv.at[1], sibling)
    send(down_hbm.at[0], down.at[pl.ds(FFL, FFL)], wsend.at[2], wrecv.at[2], sibling)

    hit0 = routes[:, 0:1] == z
    hit1 = routes[:, 1:2] == z
    hits = jnp.broadcast_to(jnp.where(hit0 | hit1, 1.0, 0.0).astype(F32), (TOK, TOK))
    weigh = jnp.where(hit0, rweight[:, 0:1], 0.0) + jnp.where(hit1, rweight[:, 1:2], 0.0)
    weigh = jnp.broadcast_to(weigh, (TOK, TOK))
    major = lax.broadcasted_iota(jnp.int32, (TOK, TOK), 0)
    minor = lax.broadcasted_iota(jnp.int32, (TOK, TOK), 1)
    token = 16 * ((z + (minor >> 4)) & 7) + 8 * h + (minor & 7)
    before = jnp.sum(jnp.where(major <= token, hits, 0.0), axis=0, keepdims=True)
    same = major == token
    named = jnp.sum(jnp.where(same, hits, 0.0), axis=0, keepdims=True)
    weight_row = jnp.sum(jnp.where(same, weigh, 0.0), axis=0, keepdims=True)
    who = major >> 6
    slot = 32 * (h + who * (1 - 2 * h)) + (major & 31)
    chosen = jnp.where(
        (((major >> 5) & 1) == ((minor >> 3) & 1)) & (before == (slot + 1).astype(F32)),
        named,
        0.0,
    )
    chooser[...] = chosen.astype(BF16)
    weight_col = jnp.broadcast_to(weight_row, (TOK, TOK)).T[:, 0:1]

    for d in range(1, NCTX):

        @pl.when(c >= d)
        def _():
            arrived(carry.at[c - d], carry_s.at[d], carry_r.at[d])

    def enter(j, state):
        return jnp.exp(carry[j, NS : NS + 1, :] * nrate) * state + carry[j, 0:NS, :]

    entering = lax.fori_loop(0, c, enter, zero_state)

    def second_pass(tb, state):
        base = pl.multiple_of(tb * 8, 8)
        dr8 = drive[pl.ds(base, 8), :]
        ins = turned(0, base)
        outw = turned(NS, base)
        for i in range(8):
            state = dec[base + i] * state + dr8[i : i + 1, :] * ins[:, i : i + 1]
            yacc[pl.ds(base + i, 1), :] = jnp.sum(
                state * outw[:, i : i + 1], axis=0, keepdims=True
            )
        return state

    lax.fori_loop(0, TOK // 8, second_pass, entering)

    gates = gate[...].astype(F32)
    yacc[...] = (yacc[...] + skip[...] * xin[...].astype(F32)) * (
        gates / (1.0 + jnp.exp(-gates))
    )

    def eights(whose):
        return jnp.concatenate(
            [
                yacc[pl.ds(pl.multiple_of(16 * lax.rem(z + d, NZ) + 8 * whose, 8), 8), :]
                for d in range(NZ)
            ],
            axis=0,
        ).astype(BF16)

    gsend[...] = eights(1 - h)
    send(gsend, gpeer, one_s.at[0], one_r.at[0], sibling)
    gmine[...] = eights(h)

    local[0].wait()
    arrived(proj.at[pl.ds(CH, CH)], wsend.at[0], wrecv.at[0])
    arrived(gpeer, one_s.at[0], one_r.at[0])

    def project(n, _):
        def block(first):
            cols = pl.ds(pl.multiple_of(first + n * 512, 512), 512)
            return jnp.dot(
                gmine[...], proj[0:CH, cols], preferred_element_type=F32
            ) + jnp.dot(gpeer[...], proj[CH : 2 * CH, cols], preferred_element_type=F32)

        both = jnp.concatenate(
            [block(0).reshape(NZ, 8, 512), block(HD).reshape(NZ, 8, 512)], axis=1
        )
        cols = pl.ds(pl.multiple_of(n * 512, 512), 512)
        own16[:, cols] = both[0]
        psend[:, :, cols] = both.astype(BF16)
        return 0

    lax.fori_loop(0, HD // 512, project, 0)
    order = (4, 3, 5, 2, 6, 1, 7)
    for d in order:
        send(psend.at[d], precv.at[d], zs1.at[d], zr1.at[d], zpeer(d))

    res = residual[...].astype(F32)
    total = own16[...] + jnp.concatenate([res[:, :HD], res[:, HD:]], axis=0)
    for d in reversed(order):
        arrived(precv.at[d], zs1.at[d], zr1.at[d])
        total = total + precv[d].astype(F32)
    upd16[...] = total
    squares = jnp.sum(total * total, axis=1, keepdims=True)
    scale = lax.rsqrt((squares[0:8] + squares[8:16]) * (1.0 / D) + 1e-05)
    gains = jnp.concatenate(
        [
            jnp.broadcast_to(gain[:, :HD], (8, HD)),
            jnp.broadcast_to(gain[:, HD:], (8, HD)),
        ],
        axis=0,
    )
    rows[0] = (total * jnp.concatenate([scale, scale], axis=0) * gains).astype(BF16)
    for d in order:
        send(rows.at[0], rows.at[NZ - d], zs2.at[d], zr2.at[d], zpeer(d))
    for d in reversed(order):
        arrived(rows.at[NZ - d], zs2.at[d], zr2.at[d])

    def select(n, _):
        cols = pl.ds(pl.multiple_of(n * 512, 512), 512)
        picked = jnp.dot(
            chooser[...], rows[:, :, cols].reshape(TOK, 512), preferred_element_type=F32
        ).astype(BF16)
        selsend[:, :, cols] = picked[64:128].reshape(2, 32, 512)
        x[0, 0, :, :, cols] = picked[0:64].reshape(2, 32, 512)
        return 0

    lax.fori_loop(0, HD // 512, select, 0)
    send(selsend, selpeer, one_s.at[1], one_r.at[1], sibling)
    arrived(selpeer, one_s.at[1], one_r.at[1])
    x[0, 0] = (x[0, 0].astype(F32) + selpeer[...].astype(F32)).astype(BF16)

    tag = [0]

    def gather(rb, ra, f, to, lb, la):
        send(
            x.at[rb, ra, f], x.at[lb, la, f], ag_s.at[tag[0]], ag_r.at[lb, la, f], to
        )
        tag[0] += 1

    def have(rb, ra, f):
        arrived(x.at[rb, ra, f], ag_s.at[0], ag_r.at[rb, ra, f])

    def along_b(ra, f):
        gather(0, ra, f, bpeer(1), 3, ra)
        gather(0, ra, f, bpeer(3), 1, ra)

    for f in range(2):
        gather(0, 0, f, apeer(1), 0, 3)
        gather(0, 0, f, apeer(3), 0, 1)
    for f in range(2):
        along_b(0, f)
    for f in range(2):
        have(0, 3, f)
        if f == 0:
            gather(0, 3, 0, apeer(1), 0, 2)
        have(0, 1, f)
        if f == 1:
            gather(0, 1, 1, apeer(3), 0, 2)
        along_b(3, f)
        along_b(1, f)

    def pass_on(ra):
        for f in range(2):
            have(3, ra, f)
            if f == 0:
                gather(3, ra, 0, bpeer(1), 2, ra)
            have(1, ra, f)
            if f == 1:
                gather(1, ra, 1, bpeer(3), 2, ra)

    for f in range(2):
        have(0, 2, f)
        along_b(2, f)
    pass_on(0)

    local[1].wait()
    local[2].wait()
    arrived(up.at[:, pl.ds(FFL, FFL)], wsend.at[1], wrecv.at[1])
    arrived(down.at[pl.ds(FFL, FFL)], wsend.at[2], wrecv.at[2])

    def experts(rb):
        def widen(n, _):
            cols = pl.ds(pl.multiple_of(n * 256, 256), 256)
            pre = jnp.dot(
                x[rb, :, 0].reshape(TOK, HD), up[0:HD, cols], preferred_element_type=F32
            ) + jnp.dot(
                x[rb, :, 1].reshape(TOK, HD), up[HD:D, cols], preferred_element_type=F32
            )
            hid[:, cols] = (pre / (1.0 + jnp.exp(-pre))).astype(BF16)
            return 0

        lax.fori_loop(0, 2 * FFL // 256, widen, 0)

        def narrow(n, _):
            cols = pl.ds(pl.multiple_of(n * 256, 256), 256)
            for f in range(2):
                wide = pl.ds(pl.multiple_of(f * HD + n * 256, 256), 256)
                part[rb, :, f, :, cols] = (
                    jnp.dot(hid[...], down[:, wide], preferred_element_type=F32)
                    .astype(BF16)
                    .reshape(4, 32, 256)
                )
            return 0

        lax.fori_loop(0, HD // 256, narrow, 0)

    experts(0)
    for ra in (3, 1, 2):
        pass_on(ra)
    experts(1)
    experts(3)

    turns = (2, 1, 3, 0)
    for ra in turns:
        send(part.at[1, ra, 1], r2.at[0, ra, 1], s2.at[0, ra, 1], r2s.at[0, ra, 1], bpeer(1))
        send(part.at[3, ra, 0], r2.at[1, ra, 0], s2.at[1, ra, 0], r2s.at[1, ra, 0], bpeer(3))
    for ra in range(4):
        for f in range(2):
            have(2, ra, f)
    experts(2)
    for ra in turns:
        send(part.at[2, ra, 0], r1.at[0, ra], s1.at[0, ra], r1s.at[0, ra], bpeer(1))
        send(part.at[2, ra, 1], r1.at[1, ra], s1.at[1, ra], r1s.at[1, ra], bpeer(3))
    for ra in turns:
        arrived(r1.at[0, ra], s1.at[0, ra], r1s.at[0, ra])
        part[1, ra, 0] = (part[1, ra, 0].astype(F32) + r1[0, ra].astype(F32)).astype(BF16)
        send(part.at[1, ra, 0], r2.at[0, ra, 0], s2.at[0, ra, 0], r2s.at[0, ra, 0], bpeer(1))
        arrived(r1.at[1, ra], s1.at[1, ra], r1s.at[1, ra])
        part[3, ra, 1] = (part[3, ra, 1].astype(F32) + r1[1, ra].astype(F32)).astype(BF16)
        send(part.at[3, ra, 1], r2.at[1, ra, 1], s2.at[1, ra, 1], r2s.at[1, ra, 1], bpeer(3))

    def along_b_sum(ra, f):
        for side in range(2):
            arrived(r2.at[side, ra, f], s2.at[side, ra, f], r2s.at[side, ra, f])
        return part[0, ra, f].astype(F32) + r2[0, ra, f].astype(F32) + r2[1, ra, f].astype(F32)

    for f in range(2):
        qsend[2, f] = along_b_sum(2, f).astype(BF16)
        send(
            qsend.at[2, f], r3.at[f], s3.at[f], r3s.at[f], apeer(1) if f == 0 else apeer(3)
        )
    for ra, early in ((1, 1), (3, 0)):
        side = 0 if ra == 1 else 1
        qsend[ra, early] = along_b_sum(ra, early).astype(BF16)
        send(
            qsend.at[ra, early],
            r4.at[side, early],
            s4.at[side, early],
            r4s.at[side, early],
            apeer(ra),
        )
    for ra, late in ((1, 0), (3, 1)):
        side = 0 if ra == 1 else 1
        summed = along_b_sum(ra, late)
        arrived(r3.at[late], s3.at[late], r3s.at[late])
        qsend[ra, late] = (summed + r3[late].astype(F32)).astype(BF16)
        send(
            qsend.at[ra, late],
            r4.at[side, late],
            s4.at[side, late],
            r4s.at[side, late],
            apeer(ra),
        )
    for f in range(2):
        q0[f] = along_b_sum(0, f)
    for f in (1, 0):
        for side in range(2):
            arrived(r4.at[side, f], s4.at[side, f], r4s.at[side, f])
        outs[0, f] = (q0[f] + r4[0, f].astype(F32) + r4[1, f].astype(F32)).astype(BF16)

    send(outs.at[0], outs.at[1], one_s.at[2], one_r.at[2], sibling)
    arrived(outs.at[1], one_s.at[2], one_r.at[2])

    def spread(n, _):
        cols = pl.ds(pl.multiple_of(n * 512, 512), 512)
        given = (
            lax.dot_general(
                chooser[...],
                outs[:, :, :, cols].reshape(TOK, 512),
                (((0,), (0,)), ((), ())),
                preferred_element_type=F32,
            )
            * weight_col
        ).reshape(NZ, 16, 512)
        own16[:, cols] = given[0]
        csend[:, :, cols] = given.astype(BF16)
        return 0

    lax.fori_loop(0, HD // 512, spread, 0)
    for d in order:
        send(csend.at[d], crecv.at[d], zs3.at[d], zr3.at[d], zpeer(d))
    total = upd16[...] + own16[...]
    for d in reversed(order):
        arrived(crecv.at[d], zs3.at[d], zr3.at[d])
        total = total + crecv[d].astype(F32)
    out[:, 0:HD] = total[0:8].astype(BF16)
    out[:, HD:D] = total[8:16].astype(BF16)

    for copy in sending:
        copy.wait_send()
    for d in range(1, NCTX):

        @pl.when(c + d < NCTX)
        def _():
            pltpu.make_async_remote_copy(
                src_ref=carry.at[c],
                dst_ref=carry.at[c],
                send_sem=carry_s.at[d],
                recv_sem=carry_r.at[d],
                device_id=sibling,
                device_id_type=pl.DeviceIdType.MESH,
            ).wait_send()


def per_device(
    residual,
    mixer_input,
    mixer_gate,
    step_size,
    decay_rate,
    state_in,
    state_out,
    skip_weight,
    projection,
    norm_gain,
    routes,
    route_weight,
    up_weight,
    down_weight,
):
    vmem = pl.BlockSpec(memory_space=pltpu.VMEM)
    hbm = pl.BlockSpec(memory_space=pl.ANY)
    dma = pltpu.SemaphoreType.DMA
    scratch = [
        pltpu.VMEM((2 * CH, D), BF16),
        pltpu.VMEM((D, 2 * FFL), BF16),
        pltpu.VMEM((2 * FFL, D), BF16),
        pltpu.VMEM((TOK, NS, CH), F32),
        pltpu.VMEM((TOK, CH), F32),
        pltpu.VMEM((TOK, CH), F32),
        pltpu.VMEM((TOK, TOK), F32),
        pltpu.VMEM((NCTX, NS + 8, CH), F32),
        pltpu.VMEM((64, CH), BF16),
        pltpu.VMEM((64, CH), BF16),
        pltpu.VMEM((64, CH), BF16),
        pltpu.VMEM((NZ, 16, HD), BF16),
        pltpu.VMEM((NZ, 16, HD), BF16),
        pltpu.VMEM((16, HD), F32),
        pltpu.VMEM((16, HD), F32),
        pltpu.VMEM((NZ, 16, HD), BF16),
        pltpu.VMEM((TOK, TOK), BF16),
        pltpu.VMEM((2, 32, HD), BF16),
        pltpu.VMEM((2, 32, HD), BF16),
        pltpu.VMEM((4, 4, 2, 32, HD), BF16),
        pltpu.VMEM((TOK, 2 * FFL), BF16),
        pltpu.VMEM((4, 4, 2, 32, HD), BF16),
        pltpu.VMEM((2, 4, 32, HD), BF16),
        pltpu.VMEM((2, 4, 2, 32, HD), BF16),
        pltpu.VMEM((2, 32, HD), BF16),
        pltpu.VMEM((2, 2, 32, HD), BF16),
        pltpu.VMEM((4, 2, 32, HD), BF16),
        pltpu.VMEM((2, 32, HD), F32),
        pltpu.VMEM((2, 2, 32, HD), BF16),
        pltpu.VMEM((NZ, 16, HD), BF16),
        pltpu.VMEM((NZ, 16, HD), BF16),
        dma((3,)),
        dma((3,)),
        dma((3,)),
        dma((NCTX,)),
        dma((NCTX,)),
        dma((3,)),
        dma((3,)),
        dma((NZ,)),
        dma((NZ,)),
        dma((NZ,)),
        dma((NZ,)),
        dma((NZ,)),
        dma((NZ,)),
        dma((40,)),
        dma((4, 4, 2)),
        dma((2, 4)),
        dma((2, 4)),
        dma((2, 4, 2)),
        dma((2, 4, 2)),
        dma((2,)),
        dma((2,)),
        dma((2, 2)),
        dma((2, 2)),
    ]
    return pl.pallas_call(
        layer_kernel,
        out_shape=jax.ShapeDtypeStruct(residual.shape, BF16),
        in_specs=[
            vmem, vmem, vmem, vmem, vmem, vmem, vmem, vmem,
            hbm, vmem, vmem, vmem, hbm, hbm,
        ],
        out_specs=vmem,
        scratch_shapes=scratch,
        compiler_params=pltpu.CompilerParams(
            collective_id=0, has_side_effects=True, vmem_limit_bytes=58 * 1024 * 1024
        ),
    )(
        residual,
        mixer_input,
        mixer_gate,
        step_size,
        decay_rate,
        state_in,
        state_out,
        skip_weight.reshape(1, CH),
        projection,
        norm_gain.reshape(1, D),
        routes,
        route_weight,
        up_weight,
        down_weight,
    )


def solution(mesh):
    in_specs = (
        P(("ctx", "exp", "half"), None),
        P("ctx", ("exp", "half")),
        P("ctx", ("exp", "half")),
        P("ctx", ("exp", "half")),
        P(None, ("exp", "half")),
        P("ctx", None),
        P("ctx", None),
        P(("exp", "half")),
        P(("exp", "half"), None),
        P(),
        P("ctx", None),
        P("ctx", None),
        P("exp", None, ("ctx", "half")),
        P("exp", ("ctx", "half"), None),
    )
    out_specs = P(("ctx", "exp", "half"), None)
    return jax.shard_map(
        per_device, mesh=mesh, in_specs=in_specs, out_specs=out_specs, check_vma=False
    )
```

profile of v0, /device:TPU:1, one launch (start us, length us, event | category | flops | bytes accessed | tf_op | source)
XLA Modules:
  0.0 138.6 jit_solution(12907148728236180150)
XLA Ops:
  0.0 1.4 %copy.15.sin = f32[128,16]{1,0:T(8,128)} copy(f32[128,16]{0,1:T(8,128)} %param.19) | data formatting | bytes 16384 | tf_op args[5]
  1.4 1.4 %copy.16.sout = f32[128,16]{1,0:T(8,128)} copy(f32[128,16]{0,1:T(8,128)} %param.20) | data formatting | bytes 16384 | tf_op args[6]
  2.8 1.4 %copy.17.routes = s32[128,2]{1,0:T(8,128)} copy(s32[128,2]{0,1:T(2,128)} %param.24) | data formatting | bytes 2048 | tf_op args[10]
  4.2 1.4 %copy.18.rweight = f32[128,2]{1,0:T(8,128)} copy(f32[128,2]{0,1:T(2,128)} %param.25) | data formatting | bytes 2048 | tf_op args[11]
  5.6 131.5 %shard_map.136 = bf16[8,4096]{1,0:T(8,128)(2,1)} custom-call(bf16[8,4096]{1,0:T(8,128)(2,1)} %residual.1, bf16[128,512]{1,0:T(8,128)(2,1)} %xin.1, bf16[128,512]{1,0:T(8,128)(2,1)} %gate.1, f32[128,512]{1,0:T(8,128)} %step.1, f32[16,512]{1,0:T(8,128)} %rate.1, f32[128,16]{1,0:T(8,128)} %copy.15.sin, f32[128,16]{1,0:T(8,128)} %copy.16.sout, ...), custom_call_target="tpu_custom_call" | custom-call | tf_op jit(solution)/shard_map/pallas_call | solution.py:590
  137.1 1.5 %copy.20 = bf16[8,4096]{1,0:T(8,128)(2,1)} copy(bf16[8,4096]{1,0:T(8,128)(2,1)} %shard_map.136) | data formatting | bytes 131072
where the time goes:
time: 139 us
  Pallas kernels  131 us (94%)
  local copies, waits for them, and re-layouts  7.11 us (5%)
    pallas_call x1, Pallas kernels, per_device(): pl.pallas_call(layer_kernel, out_shape=jax.ShapeDtypeStruct(residual.shap...  131 us
    unnamed x5, local copies, waits for them, and re-layouts  7.11 us

commit v1 on v0

v1 whole, which is shorter than its diff:
```python
import jax
import jax.numpy as jnp
from jax import lax
from jax.experimental import pallas as pl
from jax.experimental.pallas import tpu as pltpu
from jax.sharding import PartitionSpec as P

F32 = jnp.float32
BF16 = jnp.bfloat16
TOK = 128
CH = 512
NS = 16
D = 4096
FFL = 384
NZ = 8
NCTX = 16
NG = 4
W = 512


def layer_kernel(
    residual_hbm,
    xin_hbm,
    gate_hbm,
    step_hbm,
    rate_hbm,
    sin_hbm,
    sout_hbm,
    skip,
    proj_hbm,
    gain,
    routes,
    rweight,
    up_hbm,
    down_hbm,
    out,
    residual,
    xin,
    gate,
    step,
    rate,
    sin,
    sout,
    proj,
    up,
    down,
    dec,
    drive,
    yacc,
    carry,
    sums,
    gsend,
    gmine,
    gpeer,
    psend,
    rp0,
    rp,
    own16,
    upd16,
    rows,
    chooser,
    selsend,
    selpeer,
    x,
    hid,
    part,
    r1,
    r2,
    r3,
    r4,
    qsend,
    outs,
    csend,
    crecv,
    isem,
    wsem,
    wsend,
    wrecv,
    carry_s,
    carry_r,
    sum_s,
    sum_r,
    gate_s,
    gate_r,
    sel_s,
    sel_r,
    out_s,
    out_r,
    p0_s,
    p0_r,
    p_s,
    p_r,
    zs2,
    zr2,
    zs3,
    zr3,
    ag_s,
    ag_r,
    s1,
    r1s,
    s2,
    r2s,
    s3,
    r3s,
    s4,
    r4s,
):
    c = lax.axis_index("ctx")
    z = lax.axis_index("exp")
    h = lax.axis_index("half")
    sending = []

    def remote(src, dst, ssem, rsem, to):
        return pltpu.make_async_remote_copy(
            src_ref=src,
            dst_ref=dst,
            send_sem=ssem,
            recv_sem=rsem,
            device_id=to,
            device_id_type=pl.DeviceIdType.MESH,
        )

    def send(src, dst, ssem, rsem, to):
        copy = remote(src, dst, ssem, rsem, to)
        copy.start()
        sending.append(copy)

    sibling = {"ctx": c, "exp": z, "half": 1 - h}

    def arrived(dst, ssem, rsem):
        remote(dst, dst, ssem, rsem, sibling).wait_recv()

    def zpeer(d):
        return {"ctx": c, "exp": lax.rem(z + d, NZ), "half": h}

    cy, cx = lax.div(c, 4), lax.rem(c, 4)
    a = cx + h * (cy - cx)
    b = cy + h * (cx - cy)

    def ctx_at(da, db):
        return lax.rem(a + da, 4) * (1 + 3 * h) + lax.rem(b + db, 4) * (4 - 3 * h)

    def apeer(d):
        return {"ctx": ctx_at(d, 0), "exp": z, "half": h}

    def bpeer(d):
        return {"ctx": ctx_at(0, d), "exp": z, "half": h}

    inputs = [
        pltpu.make_async_copy(src, dst, isem.at[i])
        for i, (src, dst) in enumerate(
            (
                (step_hbm, step),
                (xin_hbm, xin),
                (rate_hbm, rate),
                (sin_hbm, sin),
                (sout_hbm, sout),
                (gate_hbm, gate),
                (residual_hbm, residual),
            )
        )
    ]
    local = [
        pltpu.make_async_copy(proj_hbm, proj.at[pl.ds(0, CH)], wsem.at[0]),
        pltpu.make_async_copy(up_hbm.at[0], up.at[:, pl.ds(0, FFL)], wsem.at[1]),
        pltpu.make_async_copy(down_hbm.at[0], down.at[pl.ds(0, FFL)], wsem.at[2]),
    ]
    for copy in inputs + local:
        copy.start()

    barrier = pltpu.get_barrier_semaphore()
    for d in range(1, NCTX):
        pl.semaphore_signal(
            barrier,
            inc=1,
            device_id={"ctx": lax.rem(c + d, NCTX), "exp": z, "half": h},
            device_id_type=pl.DeviceIdType.MESH,
        )
    for d in range(1, NZ):
        pl.semaphore_signal(
            barrier, inc=1, device_id=zpeer(d), device_id_type=pl.DeviceIdType.MESH
        )
    pl.semaphore_signal(
        barrier, inc=1, device_id=sibling, device_id_type=pl.DeviceIdType.MESH
    )

    for copy in inputs:
        copy.wait()
    nrate = -rate[...]
    drive[...] = step[...] * xin[...].astype(F32)
    sums[c] = jnp.sum(step[...], axis=0, keepdims=True)

    def turned(ref, base):
        return pltpu.roll(ref[...], lax.rem(TOK - base, TOK), 1)

    def first_pass(tb, state):
        base = pl.multiple_of(tb * 8, 8)
        st8 = step[pl.ds(base, 8), :]
        dr8 = drive[pl.ds(base, 8), :]
        ins = turned(sin, base)
        for i in range(8):
            decay = jnp.exp(st8[i : i + 1, :] * nrate)
            dec[base + i] = decay
            state = decay * state + dr8[i : i + 1, :] * ins[:, i : i + 1]
        return state

    zero_state = jnp.zeros((NS, CH), F32)
    carry[c] = lax.fori_loop(0, TOK // 8, first_pass, zero_state).astype(BF16)

    pl.semaphore_wait(barrier, NCTX - 1 + NZ - 1 + 1)

    def later(d):
        return {"ctx": c + d, "exp": z, "half": h}

    for d in range(1, NCTX):

        @pl.when(c + d < NCTX)
        def _():
            remote(carry.at[c], carry.at[c], carry_s.at[d], carry_r.at[d], later(d)).start()
            remote(sums.at[c], sums.at[c], sum_s.at[d], sum_r.at[d], later(d)).start()

    send(proj_hbm, proj.at[pl.ds(CH, CH)], wsend.at[0], wrecv.at[0], sibling)
    send(up_hbm.at[0], up.at[:, pl.ds(FFL, FFL)], wsend.at[1], wrecv.at[1], sibling)
    send(down_hbm.at[0], down.at[pl.ds(FFL, FFL)], wsend.at[2], wrecv.at[2], sibling)

    hit0 = routes[0:1, :] == z
    hit1 = routes[1:2, :] == z
    hits = jnp.where(hit0 | hit1, 1.0, 0.0).astype(F32)
    weigh = jnp.where(hit0, rweight[0:1, :], 0.0) + jnp.where(hit1, rweight[1:2, :], 0.0)
    hits = jnp.broadcast_to(hits, (TOK, TOK)).T
    weigh = jnp.broadcast_to(weigh, (TOK, TOK)).T
    major = lax.broadcasted_iota(jnp.int32, (TOK, TOK), 0)
    minor = lax.broadcasted_iota(jnp.int32, (TOK, TOK), 1)
    token = 16 * ((z + (minor >> 4)) & 7) + 8 * h + (minor & 7)
    before = jnp.sum(jnp.where(major <= token, hits, 0.0), axis=0, keepdims=True)
    same = major == token
    named = jnp.sum(jnp.where(same, hits, 0.0), axis=0, keepdims=True)
    weight_row = jnp.sum(jnp.where(same, weigh, 0.0), axis=0, keepdims=True)
    who = major >> 6
    slot = 32 * (h + who * (1 - 2 * h)) + (major & 31)
    chosen = jnp.where(
        (((major >> 5) & 1) == ((minor >> 3) & 1)) & (before == (slot + 1).astype(F32)),
        named,
        0.0,
    )
    chooser[...] = chosen.astype(BF16)
    weight_col = jnp.broadcast_to(weight_row, (TOK, TOK)).T[:, 0:1]

    for d in range(1, NCTX):

        @pl.when(c >= d)
        def _():
            arrived(carry.at[c - d], carry_s.at[d], carry_r.at[d])
            arrived(sums.at[c - d], sum_s.at[d], sum_r.at[d])

    def enter(j, state):
        return jnp.exp(sums[j] * nrate) * state + carry[j].astype(F32)

    entering = lax.fori_loop(0, c, enter, zero_state)

    def second_pass(tb, state):
        base = pl.multiple_of(tb * 8, 8)
        dr8 = drive[pl.ds(base, 8), :]
        ins = turned(sin, base)
        outw = turned(sout, base)
        for i in range(8):
            state = dec[base + i] * state + dr8[i : i + 1, :] * ins[:, i : i + 1]
            yacc[pl.ds(base + i, 1), :] = jnp.sum(
                state * outw[:, i : i + 1], axis=0, keepdims=True
            )
        return state

    lax.fori_loop(0, TOK // 8, second_pass, entering)

    gates = gate[...].astype(F32)
    yacc[...] = (yacc[...] + skip[...] * xin[...].astype(F32)) * (
        gates / (1.0 + jnp.exp(-gates))
    )

    def eights(whose):
        return jnp.concatenate(
            [
                yacc[pl.ds(pl.multiple_of(16 * lax.rem(z + d, NZ) + 8 * whose, 8), 8), :]
                for d in range(NZ)
            ],
            axis=0,
        ).astype(BF16)

    gsend[...] = eights(1 - h)
    send(gsend, gpeer, gate_s.at[0], gate_r.at[0], sibling)
    gmine[...] = eights(h)

    local[0].wait()
    arrived(proj.at[pl.ds(CH, CH)], wsend.at[0], wrecv.at[0])
    arrived(gpeer, gate_s.at[0], gate_r.at[0])

    def project(g, _):
        def block(f):
            cols = pl.ds(pl.multiple_of((2 * g + f) * W, W), W)
            return (
                jnp.dot(gmine[...], proj[0:CH, cols], preferred_element_type=F32)
                + jnp.dot(gpeer[...], proj[CH : 2 * CH, cols], preferred_element_type=F32)
            ).reshape(NZ, 8, W)

        both = jnp.concatenate([block(0), block(1)], axis=1)
        own16[g] = both[0]
        psend[:, g] = both.astype(BF16)
        return 0

    lax.fori_loop(0, NG, project, 0)

    def ring(way, pos, half, slot):
        send(
            psend.at[pos, pl.ds(2 * half, 2)],
            rp.at[way, slot, half],
            p_s.at[way, slot, half],
            p_r.at[way, slot, half],
            zpeer(1) if way == 0 else zpeer(NZ - 1),
        )

    def add_in(pos, half, got):
        mine = psend[pos, 2 * half : 2 * half + 2].astype(F32)
        psend[pos, 2 * half : 2 * half + 2] = (mine + got.astype(F32)).astype(BF16)

    for way in range(2):
        send(
            psend.at[4, pl.ds(2 * way, 2)],
            rp0.at[way],
            p0_s.at[way],
            p0_r.at[way],
            zpeer(1) if way == 0 else zpeer(NZ - 1),
        )
    for way in range(2):
        ring(way, 3 if way == 0 else 5, 1 - way, 0)
    for way in range(2):
        arrived(rp0.at[way], p0_s.at[way], p0_r.at[way])
        pos = 3 if way == 0 else 5
        add_in(pos, way, rp0[way])
        ring(way, pos, way, 0)
    for slot in range(2):
        for turn in range(2):
            for way in range(2):
                half = 1 - way if turn == 0 else way
                arrived(rp.at[way, slot, half], p_s.at[way, slot, half], p_r.at[way, slot, half])
                pos = 2 - slot if way == 0 else 6 + slot
                add_in(pos, half, rp[way, slot, half])
                ring(way, pos, half, slot + 1)
    squares = jnp.zeros((16, 1), F32)
    for half in range(2):
        for way in range(2):
            arrived(rp.at[way, 2, half], p_s.at[way, 2, half], p_r.at[way, 2, half])
    for g in range(NG):
        res = residual[:, 2 * W * g : 2 * W * (g + 1)].astype(F32)
        total = own16[g] + jnp.concatenate([res[:, :W], res[:, W:]], axis=0)
        for way in range(2):
            total = total + rp[way, 2, g // 2, g % 2].astype(F32)
        upd16[g] = total
        squares = squares + jnp.sum(total * total, axis=1, keepdims=True)

    scale = lax.rsqrt((squares[0:8] + squares[8:16]) * (1.0 / D) + 1e-05)
    scale = jnp.concatenate([scale, scale], axis=0)
    order = (4, 3, 5, 2, 6, 1, 7)
    for g in range(NG):
        gains = jnp.concatenate(
            [
                jnp.broadcast_to(gain[:, (2 * g + f) * W : (2 * g + f + 1) * W], (8, W))
                for f in range(2)
            ],
            axis=0,
        )
        rows[g, 0] = (upd16[g] * scale * gains).astype(BF16)
        for d in order:
            send(rows.at[g, 0], rows.at[g, NZ - d], zs2.at[g, d], zr2.at[g, d], zpeer(d))

    def select(g):
        for d in reversed(order):
            arrived(rows.at[g, NZ - d], zs2.at[g, d], zr2.at[g, d])
        picked = jnp.dot(
            chooser[...], rows[g].reshape(TOK, W), preferred_element_type=F32
        )
        selsend[g] = picked[64:128].astype(BF16).reshape(2, 32, W)
        send(selsend.at[g], selpeer.at[g], sel_s.at[g], sel_r.at[g], sibling)
        arrived(selpeer.at[g], sel_s.at[g], sel_r.at[g])
        x[0, 0, 2 * g : 2 * g + 2] = (
            picked[0:64].reshape(2, 32, W) + selpeer[g].astype(F32)
        ).astype(BF16)

    tag = [0]

    def gather(rb, ra, e, to, lb, la):
        send(x.at[rb, ra, e], x.at[lb, la, e], ag_s.at[tag[0]], ag_r.at[lb, la, e], to)
        tag[0] += 1

    def have(rb, ra, e):
        arrived(x.at[rb, ra, e], ag_s.at[0], ag_r.at[rb, ra, e])

    def along_b(ra, e):
        gather(0, ra, e, bpeer(1), 3, ra)
        gather(0, ra, e, bpeer(3), 1, ra)

    def begin(g):
        for e in (2 * g, 2 * g + 1):
            gather(0, 0, e, apeer(1), 0, 3)
            gather(0, 0, e, apeer(3), 0, 1)
        for e in (2 * g, 2 * g + 1):
            along_b(0, e)

    def neighbours(g):
        for e in (2 * g, 2 * g + 1):
            have(0, 3, e)
            if e % 2 == 0:
                gather(0, 3, e, apeer(1), 0, 2)
            have(0, 1, e)
            if e % 2 == 1:
                gather(0, 1, e, apeer(3), 0, 2)
            along_b(3, e)
            along_b(1, e)

    def opposite(g):
        for e in (2 * g, 2 * g + 1):
            have(0, 2, e)
            along_b(2, e)

    def pass_on(g, ra):
        for e in (2 * g, 2 * g + 1):
            have(3, ra, e)
            if e % 2 == 0:
                gather(3, ra, e, bpeer(1), 2, ra)
            have(1, ra, e)
            if e % 2 == 1:
                gather(1, ra, e, bpeer(3), 2, ra)

    for turn in range(NG + 3):
        if turn < NG:
            select(turn)
            begin(turn)
        if 0 <= turn - 1 < NG:
            neighbours(turn - 1)
        if 0 <= turn - 2 < NG:
            opposite(turn - 2)
            pass_on(turn - 2, 0)
        if 0 <= turn - 3 < NG:
            pass_on(turn - 3, 3)
            pass_on(turn - 3, 1)

    local[1].wait()
    local[2].wait()
    arrived(up.at[:, pl.ds(FFL, FFL)], wsend.at[1], wrecv.at[1])
    arrived(down.at[pl.ds(FFL, FFL)], wsend.at[2], wrecv.at[2])

    def widen(rb):
        def body(n, _):
            cols = pl.ds(pl.multiple_of(n * 256, 256), 256)
            pre = jnp.zeros((TOK, 256), F32)
            for e in range(2 * NG):
                pre = pre + jnp.dot(
                    x[rb, :, e].reshape(TOK, W),
                    up[e * W : (e + 1) * W, cols],
                    preferred_element_type=F32,
                )
            hid[:, cols] = (pre / (1.0 + jnp.exp(-pre))).astype(BF16)
            return 0

        lax.fori_loop(0, 2 * FFL // 256, body, 0)

    def narrow(rb, g):
        for e in (2 * g, 2 * g + 1):
            part[rb, :, e] = (
                jnp.dot(hid[...], down[:, e * W : (e + 1) * W], preferred_element_type=F32)
                .astype(BF16)
                .reshape(4, 32, W)
            )

    turns = (2, 1, 3, 0)

    def sum_b(side, ra, e):
        send(
            part.at[1 + 2 * side, ra, e],
            r2.at[side, ra, e],
            s2.at[side, ra, e],
            r2s.at[side, ra, e],
            bpeer(1 + 2 * side),
        )

    widen(0)
    for g in range(NG):
        narrow(0, g)
    for g in range(NG):
        pass_on(g, 2)
    for side in range(2):
        widen(1 + 2 * side)
        for g in range(NG):
            narrow(1 + 2 * side, g)
            for ra in turns:
                sum_b(side, ra, 2 * g + 1 - side)
    for ra in range(4):
        for e in range(2 * NG):
            have(2, ra, e)
    widen(2)
    for g in range(NG):
        narrow(2, g)
        for ra in turns:
            for side in range(2):
                send(
                    part.at[2, ra, 2 * g + side],
                    r1.at[side, ra, g],
                    s1.at[side, ra, g],
                    r1s.at[side, ra, g],
                    bpeer(1 + 2 * side),
                )

    def add_b(g):
        for ra in turns:
            for side in range(2):
                e = 2 * g + side
                arrived(r1.at[side, ra, g], s1.at[side, ra, g], r1s.at[side, ra, g])
                part[1 + 2 * side, ra, e] = (
                    part[1 + 2 * side, ra, e].astype(F32) + r1[side, ra, g].astype(F32)
                ).astype(BF16)
                sum_b(side, ra, e)

    def summed_b(ra, e):
        for side in range(2):
            arrived(r2.at[side, ra, e], s2.at[side, ra, e], r2s.at[side, ra, e])
        return part[0, ra, e].astype(F32) + r2[0, ra, e].astype(F32) + r2[1, ra, e].astype(F32)

    def sum_a(side, e):
        send(
            qsend.at[1 + 2 * side, e],
            r4.at[side, e],
            s4.at[side, e],
            r4s.at[side, e],
            apeer(1 + 2 * side),
        )

    def start_a(g):
        for side in range(2):
            e = 2 * g + side
            qsend[2, e] = summed_b(2, e).astype(BF16)
            send(qsend.at[2, e], r3.at[e], s3.at[e], r3s.at[e], apeer(1 + 2 * side))
        for side in range(2):
            e = 2 * g + 1 - side
            qsend[1 + 2 * side, e] = summed_b(1 + 2 * side, e).astype(BF16)
            sum_a(side, e)

    def add_a(g):
        for side in range(2):
            e = 2 * g + side
            total = summed_b(1 + 2 * side, e)
            arrived(r3.at[e], s3.at[e], r3s.at[e])
            qsend[1 + 2 * side, e] = (total + r3[e].astype(F32)).astype(BF16)
            sum_a(side, e)

    def finish_a(g):
        for f in range(2):
            e = 2 * g + f
            total = summed_b(0, e)
            for side in range(2):
                arrived(r4.at[side, e], s4.at[side, e], r4s.at[side, e])
                total = total + r4[side, e].astype(F32)
            outs[g, 0, f] = total.astype(BF16)
        send(outs.at[g, 0], outs.at[g, 1], out_s.at[g], out_r.at[g], sibling)

    def spread(g):
        arrived(outs.at[g, 1], out_s.at[g], out_r.at[g])
        given = (
            lax.dot_general(
                chooser[...],
                outs[g].reshape(TOK, W),
                (((0,), (0,)), ((), ())),
                preferred_element_type=F32,
            )
            * weight_col
        ).reshape(NZ, 16, W)
        upd16[g] = upd16[g] + given[0]
        csend[g] = given.astype(BF16)
        for d in order:
            send(csend.at[g, d], crecv.at[g, d], zs3.at[g, d], zr3.at[g, d], zpeer(d))

    for turn in range(NG + 4):
        if turn < NG:
            add_b(turn)
        if 0 <= turn - 1 < NG:
            start_a(turn - 1)
        if 0 <= turn - 2 < NG:
            add_a(turn - 2)
        if 0 <= turn - 3 < NG:
            finish_a(turn - 3)
        if 0 <= turn - 4 < NG:
            spread(turn - 4)
    for g in range(NG):
        total = upd16[g]
        for d in reversed(order):
            arrived(crecv.at[g, d], zs3.at[g, d], zr3.at[g, d])
            total = total + crecv[g, d].astype(F32)
        for f in range(2):
            out[:, (2 * g + f) * W : (2 * g + f + 1) * W] = total[8 * f : 8 * f + 8].astype(BF16)

    for copy in sending:
        copy.wait_send()
    for d in range(1, NCTX):

        @pl.when(c + d < NCTX)
        def _():
            remote(carry.at[c], carry.at[c], carry_s.at[d], carry_r.at[d], later(d)).wait_send()
            remote(sums.at[c], sums.at[c], sum_s.at[d], sum_r.at[d], later(d)).wait_send()


def per_device(
    residual,
    mixer_input,
    mixer_gate,
    step_size,
    decay_rate,
    state_in,
    state_out,
    skip_weight,
    projection,
    norm_gain,
    routes,
    route_weight,
    up_weight,
    down_weight,
):
    vmem = pl.BlockSpec(memory_space=pltpu.VMEM)
    hbm = pl.BlockSpec(memory_space=pl.ANY)
    dma = pltpu.SemaphoreType.DMA
    scratch = [
        pltpu.VMEM((8, D), BF16),
        pltpu.VMEM((TOK, CH), BF16),
        pltpu.VMEM((TOK, CH), BF16),
        pltpu.VMEM((TOK, CH), F32),
        pltpu.VMEM((NS, CH), F32),
        pltpu.VMEM((NS, TOK), F32),
        pltpu.VMEM((NS, TOK), F32),
        pltpu.VMEM((2 * CH, D), BF16),
        pltpu.VMEM((D, 2 * FFL), BF16),
        pltpu.VMEM((2 * FFL, D), BF16),
        pltpu.VMEM((TOK, NS, CH), F32),
        pltpu.VMEM((TOK, CH), F32),
        pltpu.VMEM((TOK, CH), F32),
        pltpu.VMEM((NCTX, NS, CH), BF16),
        pltpu.VMEM((NCTX, 1, CH), F32),
        pltpu.VMEM((64, CH), BF16),
        pltpu.VMEM((64, CH), BF16),
        pltpu.VMEM((64, CH), BF16),
        pltpu.VMEM((NZ, NG, 16, W), BF16),
        pltpu.VMEM((2, 2, 16, W), BF16),
        pltpu.VMEM((2, 3, 2, 2, 16, W), BF16),
        pltpu.VMEM((NG, 16, W), F32),
        pltpu.VMEM((NG, 16, W), F32),
        pltpu.VMEM((NG, NZ, 16, W), BF16),
        pltpu.VMEM((TOK, TOK), BF16),
        pltpu.VMEM((NG, 2, 32, W), BF16),
        pltpu.VMEM((NG, 2, 32, W), BF16),
        pltpu.VMEM((4, 4, 2 * NG, 32, W), BF16),
        pltpu.VMEM((TOK, 2 * FFL), BF16),
        pltpu.VMEM((4, 4, 2 * NG, 32, W), BF16),
        pltpu.VMEM((2, 4, NG, 32, W), BF16),
        pltpu.VMEM((2, 4, 2 * NG, 32, W), BF16),
        pltpu.VMEM((2 * NG, 32, W), BF16),
        pltpu.VMEM((2, 2 * NG, 32, W), BF16),
        pltpu.VMEM((4, 2 * NG, 32, W), BF16),
        pltpu.VMEM((NG, 2, 2, 32, W), BF16),
        pltpu.VMEM((NG, NZ, 16, W), BF16),
        pltpu.VMEM((NG, NZ, 16, W), BF16),
        dma((7,)),
        dma((3,)),
        dma((3,)),
        dma((3,)),
        dma((NCTX,)),
        dma((NCTX,)),
        dma((NCTX,)),
        dma((NCTX,)),
        dma((1,)),
        dma((1,)),
        dma((NG,)),
        dma((NG,)),
        dma((NG,)),
        dma((NG,)),
        dma((2,)),
        dma((2,)),
        dma((2, 3, 2)),
        dma((2, 3, 2)),
        dma((NG, NZ)),
        dma((NG, NZ)),
        dma((NG, NZ)),
        dma((NG, NZ)),
        dma((30 * NG,)),
        dma((4, 4, 2 * NG)),
        dma((2, 4, NG)),
        dma((2, 4, NG)),
        dma((2, 4, 2 * NG)),
        dma((2, 4, 2 * NG)),
        dma((2 * NG,)),
        dma((2 * NG,)),
        dma((2, 2 * NG)),
        dma((2, 2 * NG)),
    ]
    return pl.pallas_call(
        layer_kernel,
        out_shape=jax.ShapeDtypeStruct(residual.shape, BF16),
        in_specs=[
            hbm, hbm, hbm, hbm, hbm, hbm, hbm, vmem,
            hbm, vmem, vmem, vmem, hbm, hbm,
        ],
        out_specs=vmem,
        scratch_shapes=scratch,
        compiler_params=pltpu.CompilerParams(
            collective_id=0, has_side_effects=True, vmem_limit_bytes=58 * 1024 * 1024
        ),
    )(
        residual,
        mixer_input,
        mixer_gate,
        step_size,
        decay_rate,
        state_in.T,
        state_out.T,
        skip_weight.reshape(1, CH),
        projection,
        norm_gain.reshape(1, D),
        routes.T,
        route_weight.T,
        up_weight,
        down_weight,
    )


def solution(mesh):
    in_specs = (
        P(("ctx", "exp", "half"), None),
        P("ctx", ("exp", "half")),
        P("ctx", ("exp", "half")),
        P("ctx", ("exp", "half")),
        P(None, ("exp", "half")),
        P("ctx", None),
        P("ctx", None),
        P(("exp", "half")),
        P(("exp", "half"), None),
        P(),
        P("ctx", None),
        P("ctx", None),
        P("exp", None, ("ctx", "half")),
        P("exp", ("ctx", "half"), None),
    )
    out_specs = P(("ctx", "exp", "half"), None)
    return jax.shard_map(
        per_device, mesh=mesh, in_specs=in_specs, out_specs=out_specs, check_vma=False
    )
```

time: 139 us -> 120 us (0.86)
  Pallas kernels: 131 us -> 119 us
  local copies, waits for them, and re-layouts: 7.11 us -> 1.47 us
    pallas_call x1, Pallas kernels: 131 us -> 119 us  [per_device(): pl.pallas_call(layer_kernel, out_shape=jax.ShapeDtypeStruct(residual.shap...]
    unnamed x5 -> x1, local copies, waits for them, and re-layouts: 7.11 us -> 1.47 us
where the time goes in v1:
time: 120 us
  Pallas kernels  119 us (99%)
  local copies, waits for them, and re-layouts  1.47 us (1%)
    pallas_call x1, Pallas kernels, per_device(): pl.pallas_call(layer_kernel, out_shape=jax.ShapeDtypeStruct(residual.shap...  119 us

profile of v1, /device:TPU:1, one launch (start us, length us, event | category | flops | bytes accessed | tf_op | source)
XLA Modules:
  0.0 120.3 jit_solution(7887689039170849165)
XLA Ops:
  0.0 118.8 %shard_map.136 = bf16[8,4096]{1,0:T(8,128)(2,1)} custom-call(bf16[8,4096]{1,0:T(8,128)(2,1)} %residual_hbm.1, bf16[128,512]{1,0:T(8,128)(2,1)} %xin_hbm.1, bf16[128,512]{1,0:T(8,128)(2,1)} %gate_hbm.1, f32[128,512]{1,0:T(8,128)} %step_hbm.1, f32[16,512]{1,0:T(8,128)} %rate_hbm.1, f32[16,128]{1,0:T(8,128)} %bitcast.7, f32[16,128]{1,0:T(8,128)} %bitcast.8, ...), custom_call_target="tpu_custom_call" | custom-call | tf_op jit(solution)/shard_map/pallas_call | solution.py:700
  118.8 1.5 %copy.16 = bf16[8,4096]{1,0:T(8,128)(2,1)} copy(bf16[8,4096]{1,0:T(8,128)(2,1)} %shard_map.136) | data formatting | bytes 131072

commit v2 on v1

--- a/solution.py
+++ b/solution.py
@@ -15,7 +15,9 @@
 NZ = 8
 NCTX = 16
 NG = 4
+AHEAD = 2
 W = 512
+RZ = (0, 1, 2, 7, 6, 3, 4, 5)
 
 
 def layer_kernel(
@@ -62,11 +64,11 @@
     selsend,
     selpeer,
     x,
+    pre,
     hid,
     part,
     r1,
     r2,
-    r3,
     r4,
     qsend,
     outs,
@@ -96,20 +98,18 @@
     zr3,
     ag_s,
     ag_r,
+    ag_half,
     s1,
     r1s,
     s2,
-    r2s,
-    s3,
-    r3s,
+    r2early,
+    r2late,
     s4,
     r4s,
 ):
     c = lax.axis_index("ctx")
     z = lax.axis_index("exp")
     h = lax.axis_index("half")
-    sending = []
-
     def remote(src, dst, ssem, rsem, to):
         return pltpu.make_async_remote_copy(
             src_ref=src,
@@ -121,14 +121,15 @@
         )
 
     def send(src, dst, ssem, rsem, to):
-        copy = remote(src, dst, ssem, rsem, to)
-        copy.start()
-        sending.append(copy)
+        remote(src, dst, ssem, rsem, to).start()
 
     sibling = {"ctx": c, "exp": z, "half": 1 - h}
 
     def arrived(dst, ssem, rsem):
         remote(dst, dst, ssem, rsem, sibling).wait_recv()
+
+    def left(src, ssem):
+        remote(src, src, ssem, ssem, sibling).wait_send()
 
     def zpeer(d):
         return {"ctx": c, "exp": lax.rem(z + d, NZ), "half": h}
@@ -216,12 +217,10 @@
 
         @pl.when(c + d < NCTX)
         def _():
-            remote(carry.at[c], carry.at[c], carry_s.at[d], carry_r.at[d], later(d)).start()
-            remote(sums.at[c], sums.at[c], sum_s.at[d], sum_r.at[d], later(d)).start()
+            remote(carry.at[c], carry.at[c], carry_s.at[0], carry_r.at[0], later(d)).start()
+            remote(sums.at[c], sums.at[c], sum_s.at[0], sum_r.at[0], later(d)).start()
 
     send(proj_hbm, proj.at[pl.ds(CH, CH)], wsend.at[0], wrecv.at[0], sibling)
-    send(up_hbm.at[0], up.at[:, pl.ds(FFL, FFL)], wsend.at[1], wrecv.at[1], sibling)
-    send(down_hbm.at[0], down.at[pl.ds(FFL, FFL)], wsend.at[2], wrecv.at[2], sibling)
 
     hit0 = routes[0:1, :] == z
     hit1 = routes[1:2, :] == z
@@ -231,7 +230,9 @@
     weigh = jnp.broadcast_to(weigh, (TOK, TOK)).T
     major = lax.broadcasted_iota(jnp.int32, (TOK, TOK), 0)
     minor = lax.broadcasted_iota(jnp.int32, (TOK, TOK), 1)
-    token = 16 * ((z + (minor >> 4)) & 7) + 8 * h + (minor & 7)
+    place = minor >> 4
+    place = jnp.where(place >= 5, place - 2, jnp.where(place >= 3, 10 - place, place))
+    token = 16 * ((z + place) & 7) + 8 * h + (minor & 7)
     before = jnp.sum(jnp.where(major <= token, hits, 0.0), axis=0, keepdims=True)
     same = major == token
     named = jnp.sum(jnp.where(same, hits, 0.0), axis=0, keepdims=True)
@@ -248,10 +249,10 @@
 
     for d in range(1, NCTX):
 
-        @pl.when(c >= d)
+        @pl.when(c == d)
         def _():
-            arrived(carry.at[c - d], carry_s.at[d], carry_r.at[d])
-            arrived(sums.at[c - d], sum_s.at[d], sum_r.at[d])
+            arrived(carry.at[pl.ds(0, d)], carry_s.at[0], carry_r.at[0])
+            arrived(sums.at[pl.ds(0, d)], sum_s.at[0], sum_r.at[0])
 
     def enter(j, state):
         return jnp.exp(sums[j] * nrate) * state + carry[j].astype(F32)
@@ -288,6 +289,8 @@
 
     gsend[...] = eights(1 - h)
     send(gsend, gpeer, gate_s.at[0], gate_r.at[0], sibling)
+    send(up_hbm.at[0], up.at[:, pl.ds(FFL, FFL)], wsend.at[1], wrecv.at[1], sibling)
+    send(down_hbm.at[0], down.at[pl.ds(FFL, FFL)], wsend.at[2], wrecv.at[2], sibling)
     gmine[...] = eights(h)
 
     local[0].wait()
@@ -313,7 +316,7 @@
         send(
             psend.at[pos, pl.ds(2 * half, 2)],
             rp.at[way, slot, half],
-            p_s.at[way, slot, half],
+            p_s.at[0],
             p_r.at[way, slot, half],
             zpeer(1) if way == 0 else zpeer(NZ - 1),
         )
@@ -326,14 +329,14 @@
         send(
             psend.at[4, pl.ds(2 * way, 2)],
             rp0.at[way],
-            p0_s.at[way],
+            p0_s.at[0],
             p0_r.at[way],
             zpeer(1) if way == 0 else zpeer(NZ - 1),
         )
     for way in range(2):
         ring(way, 3 if way == 0 else 5, 1 - way, 0)
     for way in range(2):
-        arrived(rp0.at[way], p0_s.at[way], p0_r.at[way])
+        arrived(rp0.at[way], p0_s.at[0], p0_r.at[way])
         pos = 3 if way == 0 else 5
         add_in(pos, way, rp0[way])
         ring(way, pos, way, 0)
@@ -341,14 +344,14 @@
         for turn in range(2):
             for way in range(2):
                 half = 1 - way if turn == 0 else way
-                arrived(rp.at[way, slot, half], p_s.at[way, slot, half], p_r.at[way, slot, half])
+                arrived(rp.at[way, slot, half], p_s.at[0], p_r.at[way, slot, half])
                 pos = 2 - slot if way == 0 else 6 + slot
                 add_in(pos, half, rp[way, slot, half])
                 ring(way, pos, half, slot + 1)
     squares = jnp.zeros((16, 1), F32)
     for half in range(2):
         for way in range(2):
-            arrived(rp.at[way, 2, half], p_s.at[way, 2, half], p_r.at[way, 2, half])
+            arrived(rp.at[way, 2, half], p_s.at[0], p_r.at[way, 2, half])
     for g in range(NG):
         res = residual[:, 2 * W * g : 2 * W * (g + 1)].astype(F32)
         total = own16[g] + jnp.concatenate([res[:, :W], res[:, W:]], axis=0)
@@ -359,7 +362,19 @@
 
     scale = lax.rsqrt((squares[0:8] + squares[8:16]) * (1.0 / D) + 1e-05)
     scale = jnp.concatenate([scale, scale], axis=0)
-    order = (4, 3, 5, 2, 6, 1, 7)
+    far_first = (6, 5, 7, 4, 2, 3, 1)
+
+    def send_rows(g):
+        for i in far_first:
+            near = 0 if RZ.index(NZ - RZ[i]) < 5 else 1
+            send(
+                rows.at[0, g],
+                rows.at[RZ.index(NZ - RZ[i]), g],
+                zs2.at[0],
+                zr2.at[g, near],
+                zpeer(RZ[i]),
+            )
+
     for g in range(NG):
         gains = jnp.concatenate(
             [
@@ -368,100 +383,94 @@
             ],
             axis=0,
         )
-        rows[g, 0] = (upd16[g] * scale * gains).astype(BF16)
-        for d in order:
-            send(rows.at[g, 0], rows.at[g, NZ - d], zs2.at[g, d], zr2.at[g, d], zpeer(d))
+        rows[0, g] = (upd16[g] * scale * gains).astype(BF16)
+        if g < AHEAD:
+            send_rows(g)
 
     def select(g):
-        for d in reversed(order):
-            arrived(rows.at[g, NZ - d], zs2.at[g, d], zr2.at[g, d])
+        arrived(rows.at[pl.ds(1, 4), g], zs2.at[0], zr2.at[g, 0])
+        if g + AHEAD < NG:
+            send_rows(g + AHEAD)
+        arrived(rows.at[pl.ds(5, 3), g], zs2.at[0], zr2.at[g, 1])
         picked = jnp.dot(
-            chooser[...], rows[g].reshape(TOK, W), preferred_element_type=F32
+            chooser[...], rows[:, g].reshape(TOK, W), preferred_element_type=F32
         )
         selsend[g] = picked[64:128].astype(BF16).reshape(2, 32, W)
-        send(selsend.at[g], selpeer.at[g], sel_s.at[g], sel_r.at[g], sibling)
-        arrived(selpeer.at[g], sel_s.at[g], sel_r.at[g])
-        x[0, 0, 2 * g : 2 * g + 2] = (
+        send(selsend.at[g], selpeer.at[g], sel_s.at[0], sel_r.at[g], sibling)
+        arrived(selpeer.at[g], sel_s.at[0], sel_r.at[g])
+        x[0, 2 * g : 2 * g + 2] = (
             picked[0:64].reshape(2, 32, W) + selpeer[g].astype(F32)
         ).astype(BF16)
 
-    tag = [0]
-
-    def gather(rb, ra, e, to, lb, la):
-        send(x.at[rb, ra, e], x.at[lb, la, e], ag_s.at[tag[0]], ag_r.at[lb, la, e], to)
-        tag[0] += 1
-
-    def have(rb, ra, e):
-        arrived(x.at[rb, ra, e], ag_s.at[0], ag_r.at[rb, ra, e])
-
-    def along_b(ra, e):
-        gather(0, ra, e, bpeer(1), 3, ra)
-        gather(0, ra, e, bpeer(3), 1, ra)
+    def pair(g):
+        return pl.ds(2 * g, 2)
+
+    def ready(rb, ra, g):
+        return ag_r.at[(8 if rb == 3 else 4 * rb) + ra, g]
+
+    def gather(ra, g, to, lb, la):
+        send(x.at[ra, pair(g)], x.at[4 * lb + la, pair(g)], ag_s.at[0], ready(lb, la, g), to)
+
+    def have(rb, ra, g):
+        arrived(x.at[4 * rb + ra, pair(g)], ag_s.at[0], ready(rb, ra, g))
+
+    def along_b(ra, g):
+        gather(ra, g, bpeer(1), 3, ra)
+        gather(ra, g, bpeer(3), 1, ra)
 
     def begin(g):
-        for e in (2 * g, 2 * g + 1):
-            gather(0, 0, e, apeer(1), 0, 3)
-            gather(0, 0, e, apeer(3), 0, 1)
-        for e in (2 * g, 2 * g + 1):
-            along_b(0, e)
+        for d in (2, 1, 3):
+            gather(0, g, apeer(d), 0, 4 - d)
+        along_b(0, g)
 
     def neighbours(g):
-        for e in (2 * g, 2 * g + 1):
-            have(0, 3, e)
-            if e % 2 == 0:
-                gather(0, 3, e, apeer(1), 0, 2)
-            have(0, 1, e)
-            if e % 2 == 1:
-                gather(0, 1, e, apeer(3), 0, 2)
-            along_b(3, e)
-            along_b(1, e)
-
-    def opposite(g):
-        for e in (2 * g, 2 * g + 1):
-            have(0, 2, e)
-            along_b(2, e)
-
-    def pass_on(g, ra):
-        for e in (2 * g, 2 * g + 1):
-            have(3, ra, e)
-            if e % 2 == 0:
-                gather(3, ra, e, bpeer(1), 2, ra)
-            have(1, ra, e)
-            if e % 2 == 1:
-                gather(1, ra, e, bpeer(3), 2, ra)
-
-    for turn in range(NG + 3):
-        if turn < NG:
-            select(turn)
-            begin(turn)
-        if 0 <= turn - 1 < NG:
+        for ra in (3, 1, 2):
+            have(0, ra, g)
+            along_b(ra, g)
+
+    def pass_on(g):
+        for ra in (0, 3, 1, 2):
+            for side in range(2):
+                rb, e = 3 - 2 * side, 2 * g + side
+                have(rb, ra, g)
+                send(
+                    x.at[4 * rb + ra, e],
+                    x.at[8 + ra, e],
+                    ag_s.at[0],
+                    ag_half.at[ra, e],
+                    bpeer(1 + 2 * side),
+                )
+
+    def widen(rb, g):
+        wide = jnp.concatenate(
+            [x[4 * rb : 4 * rb + 4, e].reshape(TOK, W) for e in (2 * g, 2 * g + 1)], axis=1
+        )
+        got = jnp.dot(wide, up[2 * g * W : 2 * (g + 1) * W, :], preferred_element_type=F32)
+        if g == 0:
+            pre[rb] = got
+        elif g < NG - 1:
+            pre[rb] = pre[rb] + got
+        else:
+            got = pre[rb] + got
+            hid[...] = (got / (1.0 + jnp.exp(-got))).astype(BF16)
+
+    for turn in range(NG):
+        select(turn)
+        begin(turn)
+        if turn == 0:
+            local[1].wait()
+            local[2].wait()
+            arrived(up.at[:, pl.ds(FFL, FFL)], wsend.at[1], wrecv.at[1])
+            arrived(down.at[pl.ds(FFL, FFL)], wsend.at[2], wrecv.at[2])
+        if turn >= 1:
             neighbours(turn - 1)
-        if 0 <= turn - 2 < NG:
-            opposite(turn - 2)
-            pass_on(turn - 2, 0)
-        if 0 <= turn - 3 < NG:
-            pass_on(turn - 3, 3)
-            pass_on(turn - 3, 1)
-
-    local[1].wait()
-    local[2].wait()
-    arrived(up.at[:, pl.ds(FFL, FFL)], wsend.at[1], wrecv.at[1])
-    arrived(down.at[pl.ds(FFL, FFL)], wsend.at[2], wrecv.at[2])
-
-    def widen(rb):
-        def body(n, _):
-            cols = pl.ds(pl.multiple_of(n * 256, 256), 256)
-            pre = jnp.zeros((TOK, 256), F32)
-            for e in range(2 * NG):
-                pre = pre + jnp.dot(
-                    x[rb, :, e].reshape(TOK, W),
-                    up[e * W : (e + 1) * W, cols],
-                    preferred_element_type=F32,
-                )
-            hid[:, cols] = (pre / (1.0 + jnp.exp(-pre))).astype(BF16)
-            return 0
-
-        lax.fori_loop(0, 2 * FFL // 256, body, 0)
+            widen(0, turn - 1)
+        if turn >= 2:
+            pass_on(turn - 2)
+            widen(1, turn - 2)
+            widen(3, turn - 2)
+    neighbours(NG - 1)
+    pass_on(NG - 2)
 
     def narrow(rb, g):
         for e in (2 * g, 2 * g + 1):
@@ -472,97 +481,88 @@
             )
 
     turns = (2, 1, 3, 0)
-
-    def sum_b(side, ra, e):
-        send(
-            part.at[1 + 2 * side, ra, e],
-            r2.at[side, ra, e],
-            s2.at[side, ra, e],
-            r2s.at[side, ra, e],
-            bpeer(1 + 2 * side),
-        )
-
-    widen(0)
+    widen(0, NG - 1)
     for g in range(NG):
         narrow(0, g)
+    widen(1, NG - 2)
+    widen(3, NG - 2)
+    pass_on(NG - 1)
+    for side in range(2):
+        widen(1 + 2 * side, NG - 1)
+        for g in range(NG):
+            e = 2 * g + 1 - side
+            narrow(1 + 2 * side, g)
+            send(
+                part.at[1 + 2 * side, pl.ds(0, 4), e],
+                r2.at[side, pl.ds(0, 4), e],
+                s2.at[0],
+                r2early.at[side, g],
+                bpeer(1 + 2 * side),
+            )
     for g in range(NG):
-        pass_on(g, 2)
-    for side in range(2):
-        widen(1 + 2 * side)
-        for g in range(NG):
-            narrow(1 + 2 * side, g)
-            for ra in turns:
-                sum_b(side, ra, 2 * g + 1 - side)
-    for ra in range(4):
-        for e in range(2 * NG):
-            have(2, ra, e)
-    widen(2)
+        for ra in range(4):
+            for e in (2 * g, 2 * g + 1):
+                arrived(x.at[8 + ra, e], ag_s.at[0], ag_half.at[ra, e])
+        widen(2, g)
     for g in range(NG):
         narrow(2, g)
-        for ra in turns:
-            for side in range(2):
-                send(
-                    part.at[2, ra, 2 * g + side],
-                    r1.at[side, ra, g],
-                    s1.at[side, ra, g],
-                    r1s.at[side, ra, g],
-                    bpeer(1 + 2 * side),
-                )
+        for side in range(2):
+            send(
+                part.at[2, pl.ds(0, 4), 2 * g + side],
+                r1.at[side, pl.ds(0, 4), g],
+                s1.at[0],
+                r1s.at[side, g],
+                bpeer(1 + 2 * side),
+            )
 
     def add_b(g):
+        for side in range(2):
+            arrived(r1.at[side, pl.ds(0, 4), g], s1.at[0], r1s.at[side, g])
         for ra in turns:
             for side in range(2):
                 e = 2 * g + side
-                arrived(r1.at[side, ra, g], s1.at[side, ra, g], r1s.at[side, ra, g])
                 part[1 + 2 * side, ra, e] = (
                     part[1 + 2 * side, ra, e].astype(F32) + r1[side, ra, g].astype(F32)
                 ).astype(BF16)
-                sum_b(side, ra, e)
-
-    def summed_b(ra, e):
+                send(
+                    part.at[1 + 2 * side, ra, e],
+                    r2.at[side, ra, e],
+                    s2.at[0],
+                    r2late.at[side, ra, g],
+                    bpeer(1 + 2 * side),
+                )
+
+    def summed_b(ra, g):
+        total = part[0, ra, 2 * g : 2 * g + 2].astype(F32)
         for side in range(2):
-            arrived(r2.at[side, ra, e], s2.at[side, ra, e], r2s.at[side, ra, e])
-        return part[0, ra, e].astype(F32) + r2[0, ra, e].astype(F32) + r2[1, ra, e].astype(F32)
-
-    def sum_a(side, e):
-        send(
-            qsend.at[1 + 2 * side, e],
-            r4.at[side, e],
-            s4.at[side, e],
-            r4s.at[side, e],
-            apeer(1 + 2 * side),
-        )
+            arrived(r2.at[side, ra, 2 * g + side], s2.at[0], r2late.at[side, ra, g])
+            total = total + r2[side, ra, 2 * g : 2 * g + 2].astype(F32)
+        return total
 
     def start_a(g):
         for side in range(2):
-            e = 2 * g + side
-            qsend[2, e] = summed_b(2, e).astype(BF16)
-            send(qsend.at[2, e], r3.at[e], s3.at[e], r3s.at[e], apeer(1 + 2 * side))
-        for side in range(2):
             e = 2 * g + 1 - side
-            qsend[1 + 2 * side, e] = summed_b(1 + 2 * side, e).astype(BF16)
-            sum_a(side, e)
-
-    def add_a(g):
-        for side in range(2):
-            e = 2 * g + side
-            total = summed_b(1 + 2 * side, e)
-            arrived(r3.at[e], s3.at[e], r3s.at[e])
-            qsend[1 + 2 * side, e] = (total + r3[e].astype(F32)).astype(BF16)
-            sum_a(side, e)
+            arrived(r2.at[side, pl.ds(0, 4), e], s2.at[0], r2early.at[side, g])
+        for ra in (2, 1, 3):
+            qsend[ra - 1, 2 * g : 2 * g + 2] = summed_b(ra, g).astype(BF16)
+            send(
+                qsend.at[ra - 1, pair(g)],
+                r4.at[ra - 1, pair(g)],
+                s4.at[0],
+                r4s.at[ra - 1, g],
+                apeer(ra),
+            )
 
     def finish_a(g):
-        for f in range(2):
-            e = 2 * g + f
-            total = summed_b(0, e)
-            for side in range(2):
-                arrived(r4.at[side, e], s4.at[side, e], r4s.at[side, e])
-                total = total + r4[side, e].astype(F32)
-            outs[g, 0, f] = total.astype(BF16)
-        send(outs.at[g, 0], outs.at[g, 1], out_s.at[g], out_r.at[g], sibling)
+        total = summed_b(0, g)
+        for i in range(3):
+            arrived(r4.at[i, pair(g)], s4.at[0], r4s.at[i, g])
+            total = total + r4[i, 2 * g : 2 * g + 2].astype(F32)
+        outs[g, 0] = total.astype(BF16)
+        send(outs.at[g, 0], outs.at[g, 1], out_s.at[0], out_r.at[g], sibling)
 
     def spread(g):
-        arrived(outs.at[g, 1], out_s.at[g], out_r.at[g])
+        arrived(outs.at[g, 1], out_s.at[0], out_r.at[g])
         given = (
             lax.dot_general(
                 chooser[...],
@@ -573,37 +573,48 @@
             * weight_col
         ).reshape(NZ, 16, W)
         upd16[g] = upd16[g] + given[0]
-        csend[g] = given.astype(BF16)
-        for d in order:
-            send(csend.at[g, d], crecv.at[g, d], zs3.at[g, d], zr3.at[g, d], zpeer(d))
-
-    for turn in range(NG + 4):
+        csend[:, g] = given.astype(BF16)
+        for i in far_first:
+            send(csend.at[i, g], crecv.at[i, g], zs3.at[0], zr3.at[g], zpeer(RZ[i]))
+
+    for g in range(NG):
+        add_b(g)
+    for turn in range(NG + 3):
         if turn < NG:
-            add_b(turn)
-        if 0 <= turn - 1 < NG:
-            start_a(turn - 1)
+            start_a(turn)
         if 0 <= turn - 2 < NG:
-            add_a(turn - 2)
+            finish_a(turn - 2)
         if 0 <= turn - 3 < NG:
-            finish_a(turn - 3)
-        if 0 <= turn - 4 < NG:
-            spread(turn - 4)
+            spread(turn - 3)
     for g in range(NG):
+        arrived(crecv.at[pl.ds(1, NZ - 1), g], zs3.at[0], zr3.at[g])
         total = upd16[g]
-        for d in reversed(order):
-            arrived(crecv.at[g, d], zs3.at[g, d], zr3.at[g, d])
-            total = total + crecv[g, d].astype(F32)
+        for i in range(1, NZ):
+            total = total + crecv[i, g].astype(F32)
         for f in range(2):
             out[:, (2 * g + f) * W : (2 * g + f + 1) * W] = total[8 * f : 8 * f + 8].astype(BF16)
 
-    for copy in sending:
-        copy.wait_send()
+    left(proj.at[pl.ds(0, CH)], wsend.at[0])
+    left(up.at[:, pl.ds(0, FFL)], wsend.at[1])
+    left(down.at[pl.ds(0, FFL)], wsend.at[2])
     for d in range(1, NCTX):
 
-        @pl.when(c + d < NCTX)
+        @pl.when(c + d == NCTX - 1)
         def _():
-            remote(carry.at[c], carry.at[c], carry_s.at[d], carry_r.at[d], later(d)).wait_send()
-            remote(sums.at[c], sums.at[c], sum_s.at[d], sum_r.at[d], later(d)).wait_send()
+            left(carry.at[pl.ds(0, d)], carry_s.at[0])
+            left(sums.at[pl.ds(0, d)], sum_s.at[0])
+
+    left(gsend, gate_s.at[0])
+    left(rp0, p0_s.at[0])
+    left(rp, p_s.at[0])
+    left(rows.at[pl.ds(1, NZ - 1)], zs2.at[0])
+    left(selsend, sel_s.at[0])
+    left(x.at[pl.ds(0, 15)], ag_s.at[0])
+    left(r1, s1.at[0])
+    left(r2, s2.at[0])
+    left(r4, s4.at[0])
+    left(selsend, out_s.at[0])
+    left(crecv.at[pl.ds(1, NZ - 1)], zs3.at[0])
 
 
 def per_device(
@@ -649,53 +660,53 @@
         pltpu.VMEM((2, 3, 2, 2, 16, W), BF16),
         pltpu.VMEM((NG, 16, W), F32),
         pltpu.VMEM((NG, 16, W), F32),
-        pltpu.VMEM((NG, NZ, 16, W), BF16),
+        pltpu.VMEM((NZ, NG, 16, W), BF16),
         pltpu.VMEM((TOK, TOK), BF16),
         pltpu.VMEM((NG, 2, 32, W), BF16),
         pltpu.VMEM((NG, 2, 32, W), BF16),
-        pltpu.VMEM((4, 4, 2 * NG, 32, W), BF16),
+        pltpu.VMEM((16, 2 * NG, 32, W), BF16),
+        pltpu.VMEM((4, TOK, 2 * FFL), F32),
         pltpu.VMEM((TOK, 2 * FFL), BF16),
         pltpu.VMEM((4, 4, 2 * NG, 32, W), BF16),
         pltpu.VMEM((2, 4, NG, 32, W), BF16),
         pltpu.VMEM((2, 4, 2 * NG, 32, W), BF16),
-        pltpu.VMEM((2 * NG, 32, W), BF16),
-        pltpu.VMEM((2, 2 * NG, 32, W), BF16),
-        pltpu.VMEM((4, 2 * NG, 32, W), BF16),
+        pltpu.VMEM((3, 2 * NG, 32, W), BF16),
+        pltpu.VMEM((3, 2 * NG, 32, W), BF16),
         pltpu.VMEM((NG, 2, 2, 32, W), BF16),
-        pltpu.VMEM((NG, NZ, 16, W), BF16),
-        pltpu.VMEM((NG, NZ, 16, W), BF16),
+        pltpu.VMEM((NZ, NG, 16, W), BF16),
+        pltpu.VMEM((NZ, NG, 16, W), BF16),
         dma((7,)),
         dma((3,)),
         dma((3,)),
         dma((3,)),
-        dma((NCTX,)),
-        dma((NCTX,)),
-        dma((NCTX,)),
-        dma((NCTX,)),
+        dma((1,)),
+        dma((1,)),
+        dma((1,)),
+        dma((1,)),
+        dma((1,)),
         dma((1,)),
         dma((1,)),
         dma((NG,)),
+        dma((1,)),
         dma((NG,)),
+        dma((1,)),
+        dma((2,)),
+        dma((1,)),
+        dma((2, 3, 2)),
+        dma((1,)),
+        dma((NG, 2)),
+        dma((1,)),
         dma((NG,)),
-        dma((NG,)),
-        dma((2,)),
-        dma((2,)),
-        dma((2, 3, 2)),
-        dma((2, 3, 2)),
-        dma((NG, NZ)),
-        dma((NG, NZ)),
-        dma((NG, NZ)),
-        dma((NG, NZ)),
-        dma((30 * NG,)),
-        dma((4, 4, 2 * NG)),
+        dma((1,)),
+        dma((12, NG)),
+        dma((4, 2 * NG)),
+        dma((1,)),
+        dma((2, NG)),
+        dma((1,)),
+        dma((2, NG)),
         dma((2, 4, NG)),
-        dma((2, 4, NG)),
-        dma((2, 4, 2 * NG)),
-        dma((2, 4, 2 * NG)),
-        dma((2 * NG,)),
-        dma((2 * NG,)),
-        dma((2, 2 * NG)),
-        dma((2, 2 * NG)),
+        dma((1,)),
+        dma((3, NG)),
     ]
     return pl.pallas_call(
         layer_kernel,

time: 120 us -> 112 us (0.933)
  Pallas kernels: 119 us -> 110 us
    pallas_call x1, Pallas kernels: 119 us -> 110 us  [per_device(): pl.pallas_call(layer_kernel, out_shape=jax.ShapeDtypeStruct(residual.shap...]
where the time goes in v2:
time: 112 us
  Pallas kernels  110 us (98%)
  local copies, waits for them, and re-layouts  1.47 us (1%)
    pallas_call x1, Pallas kernels, per_device(): pl.pallas_call(layer_kernel, out_shape=jax.ShapeDtypeStruct(residual.shap...  110 us

profile of v2, /device:TPU:1, one launch (start us, length us, event | category | flops | bytes accessed | tf_op | source)
XLA Modules:
  0.0 111.7 jit_solution(16173452951219899777)
XLA Ops:
  0.0 110.2 %shard_map.136 = bf16[8,4096]{1,0:T(8,128)(2,1)} custom-call(bf16[8,4096]{1,0:T(8,128)(2,1)} %residual_hbm.1, bf16[128,512]{1,0:T(8,128)(2,1)} %xin_hbm.1, bf16[128,512]{1,0:T(8,128)(2,1)} %gate_hbm.1, f32[128,512]{1,0:T(8,128)} %step_hbm.1, f32[16,512]{1,0:T(8,128)} %rate_hbm.1, f32[16,128]{1,0:T(8,128)} %bitcast.7, f32[16,128]{1,0:T(8,128)} %bitcast.8, ...), custom_call_target="tpu_custom_call" | custom-call | tf_op jit(solution)/shard_map/pallas_call | solution.py:711
  110.2 1.5 %copy.16 = bf16[8,4096]{1,0:T(8,128)(2,1)} copy(bf16[8,4096]{1,0:T(8,128)(2,1)} %shard_map.136) | data formatting | bytes 131072

commit v3 on v2

--- a/solution.py
+++ b/solution.py
@@ -312,51 +312,36 @@
 
     lax.fori_loop(0, NG, project, 0)
 
-    def ring(way, pos, half, slot):
-        send(
-            psend.at[pos, pl.ds(2 * half, 2)],
-            rp.at[way, slot, half],
-            p_s.at[0],
-            p_r.at[way, slot, half],
-            zpeer(1) if way == 0 else zpeer(NZ - 1),
-        )
-
-    def add_in(pos, half, got):
-        mine = psend[pos, 2 * half : 2 * half + 2].astype(F32)
-        psend[pos, 2 * half : 2 * half + 2] = (mine + got.astype(F32)).astype(BF16)
-
     for way in range(2):
         send(
             psend.at[4, pl.ds(2 * way, 2)],
             rp0.at[way],
             p0_s.at[0],
             p0_r.at[way],
-            zpeer(1) if way == 0 else zpeer(NZ - 1),
+            zpeer((2, 6)[way]),
         )
+        send(psend.at[(3, 5)[way]], rp.at[way, 0], p_s.at[0], p_r.at[way, 0], zpeer((1, 7)[way]))
     for way in range(2):
-        ring(way, 3 if way == 0 else 5, 1 - way, 0)
+        send(psend.at[(1, 7)[way]], rp.at[way, 1], p_s.at[0], p_r.at[way, 1], zpeer((1, 7)[way]))
     for way in range(2):
+        pos = (2, 6)[way]
+        arrived(rp.at[way, 0], p_s.at[0], p_r.at[way, 0])
         arrived(rp0.at[way], p0_s.at[0], p0_r.at[way])
-        pos = 3 if way == 0 else 5
-        add_in(pos, way, rp0[way])
-        ring(way, pos, way, 0)
-    for slot in range(2):
-        for turn in range(2):
-            for way in range(2):
-                half = 1 - way if turn == 0 else way
-                arrived(rp.at[way, slot, half], p_s.at[0], p_r.at[way, slot, half])
-                pos = 2 - slot if way == 0 else 6 + slot
-                add_in(pos, half, rp[way, slot, half])
-                ring(way, pos, half, slot + 1)
+        for g in range(NG):
+            total = psend[pos, g].astype(F32) + rp[way, 0, g].astype(F32)
+            if g // 2 == way:
+                total = total + rp0[way, g % 2].astype(F32)
+            psend[pos, g] = total.astype(BF16)
+        send(psend.at[pos], rp.at[way, 2], p_s.at[0], p_r.at[way, 2], zpeer(pos))
+    for way in range(2):
+        for slot in (1, 2):
+            arrived(rp.at[way, slot], p_s.at[0], p_r.at[way, slot])
     squares = jnp.zeros((16, 1), F32)
-    for half in range(2):
-        for way in range(2):
-            arrived(rp.at[way, 2, half], p_s.at[0], p_r.at[way, 2, half])
     for g in range(NG):
         res = residual[:, 2 * W * g : 2 * W * (g + 1)].astype(F32)
         total = own16[g] + jnp.concatenate([res[:, :W], res[:, W:]], axis=0)
         for way in range(2):
-            total = total + rp[way, 2, g // 2, g % 2].astype(F32)
+            total = total + rp[way, 1, g].astype(F32) + rp[way, 2, g].astype(F32)
         upd16[g] = total
         squares = squares + jnp.sum(total * total, axis=1, keepdims=True)
 
@@ -480,7 +465,6 @@
                 .reshape(4, 32, W)
             )
 
-    turns = (2, 1, 3, 0)
     widen(0, NG - 1)
     for g in range(NG):
         narrow(0, g)
@@ -518,24 +502,22 @@
     def add_b(g):
         for side in range(2):
             arrived(r1.at[side, pl.ds(0, 4), g], s1.at[0], r1s.at[side, g])
-        for ra in turns:
-            for side in range(2):
-                e = 2 * g + side
-                part[1 + 2 * side, ra, e] = (
-                    part[1 + 2 * side, ra, e].astype(F32) + r1[side, ra, g].astype(F32)
-                ).astype(BF16)
-                send(
-                    part.at[1 + 2 * side, ra, e],
-                    r2.at[side, ra, e],
-                    s2.at[0],
-                    r2late.at[side, ra, g],
-                    bpeer(1 + 2 * side),
-                )
+        for side in range(2):
+            e = 2 * g + side
+            part[1 + 2 * side, :, e] = (
+                part[1 + 2 * side, :, e].astype(F32) + r1[side, :, g].astype(F32)
+            ).astype(BF16)
+            send(
+                part.at[1 + 2 * side, pl.ds(0, 4), e],
+                r2.at[side, pl.ds(0, 4), e],
+                s2.at[0],
+                r2late.at[side, g],
+                bpeer(1 + 2 * side),
+            )
 
     def summed_b(ra, g):
         total = part[0, ra, 2 * g : 2 * g + 2].astype(F32)
         for side in range(2):
-            arrived(r2.at[side, ra, 2 * g + side], s2.at[0], r2late.at[side, ra, g])
             total = total + r2[side, ra, 2 * g : 2 * g + 2].astype(F32)
         return total
 
@@ -543,6 +525,8 @@
         for side in range(2):
             e = 2 * g + 1 - side
             arrived(r2.at[side, pl.ds(0, 4), e], s2.at[0], r2early.at[side, g])
+            e = 2 * g + side
+            arrived(r2.at[side, pl.ds(0, 4), e], s2.at[0], r2late.at[side, g])
         for ra in (2, 1, 3):
             qsend[ra - 1, 2 * g : 2 * g + 2] = summed_b(ra, g).astype(BF16)
             send(
@@ -657,7 +641,7 @@
         pltpu.VMEM((64, CH), BF16),
         pltpu.VMEM((NZ, NG, 16, W), BF16),
         pltpu.VMEM((2, 2, 16, W), BF16),
-        pltpu.VMEM((2, 3, 2, 2, 16, W), BF16),
+        pltpu.VMEM((2, 3, NG, 16, W), BF16),
         pltpu.VMEM((NG, 16, W), F32),
         pltpu.VMEM((NG, 16, W), F32),
         pltpu.VMEM((NZ, NG, 16, W), BF16),
@@ -692,7 +676,7 @@
         dma((1,)),
         dma((2,)),
         dma((1,)),
-        dma((2, 3, 2)),
+        dma((2, 3)),
         dma((1,)),
         dma((NG, 2)),
         dma((1,)),
@@ -704,7 +688,7 @@
         dma((2, NG)),
         dma((1,)),
         dma((2, NG)),
-        dma((2, 4, NG)),
+        dma((2, NG)),
         dma((1,)),
         dma((3, NG)),
     ]

time: 112 us -> 110 us (0.982)
    pallas_call x1, Pallas kernels: 110 us -> 109 us  [per_device(): pl.pallas_call(layer_kernel, out_shape=jax.ShapeDtypeStruct(residual.shap...]
where the time goes in v3:
time: 110 us
  Pallas kernels  109 us (99%)
  local copies, waits for them, and re-layouts  1.47 us (1%)
    pallas_call x1, Pallas kernels, per_device(): pl.pallas_call(layer_kernel, out_shape=jax.ShapeDtypeStruct(residual.shap...  109 us

profile of v3, /device:TPU:1, one launch (start us, length us, event | category | flops | bytes accessed | tf_op | source)
XLA Modules:
  0.0 110.1 jit_solution(17355961910180121101)
XLA Ops:
  0.0 108.6 %shard_map.136 = bf16[8,4096]{1,0:T(8,128)(2,1)} custom-call(bf16[8,4096]{1,0:T(8,128)(2,1)} %residual_hbm.1, bf16[128,512]{1,0:T(8,128)(2,1)} %xin_hbm.1, bf16[128,512]{1,0:T(8,128)(2,1)} %gate_hbm.1, f32[128,512]{1,0:T(8,128)} %step_hbm.1, f32[16,512]{1,0:T(8,128)} %rate_hbm.1, f32[16,128]{1,0:T(8,128)} %bitcast.7, f32[16,128]{1,0:T(8,128)} %bitcast.8, ...), custom_call_target="tpu_custom_call" | custom-call | tf_op jit(solution)/shard_map/pallas_call | solution.py:695
  108.6 1.5 %copy.16 = bf16[8,4096]{1,0:T(8,128)(2,1)} copy(bf16[8,4096]{1,0:T(8,128)(2,1)} %shard_map.136) | data formatting | bytes 131072

commit v4 on v3

--- a/solution.py
+++ b/solution.py
@@ -54,6 +54,7 @@
     gsend,
     gmine,
     gpeer,
+    half,
     psend,
     rp0,
     rp,
@@ -293,16 +294,23 @@
     send(down_hbm.at[0], down.at[pl.ds(FFL, FFL)], wsend.at[2], wrecv.at[2], sibling)
     gmine[...] = eights(h)
 
-    local[0].wait()
-    arrived(proj.at[pl.ds(CH, CH)], wsend.at[0], wrecv.at[0])
-    arrived(gpeer, gate_s.at[0], gate_r.at[0])
+    def columns(g, f):
+        return pl.ds(pl.multiple_of((2 * g + f) * W, W), W)
+
+    def project_mine(g, _):
+        for f in range(2):
+            half[g, f] = jnp.dot(
+                gmine[...], proj[0:CH, columns(g, f)], preferred_element_type=F32
+            )
+        return 0
 
     def project(g, _):
         def block(f):
-            cols = pl.ds(pl.multiple_of((2 * g + f) * W, W), W)
             return (
-                jnp.dot(gmine[...], proj[0:CH, cols], preferred_element_type=F32)
-                + jnp.dot(gpeer[...], proj[CH : 2 * CH, cols], preferred_element_type=F32)
+                half[g, f]
+                + jnp.dot(
+                    gpeer[...], proj[CH : 2 * CH, columns(g, f)], preferred_element_type=F32
+                )
             ).reshape(NZ, 8, W)
 
         both = jnp.concatenate([block(0), block(1)], axis=1)
@@ -310,6 +318,10 @@
         psend[:, g] = both.astype(BF16)
         return 0
 
+    local[0].wait()
+    lax.fori_loop(0, NG, project_mine, 0)
+    arrived(proj.at[pl.ds(CH, CH)], wsend.at[0], wrecv.at[0])
+    arrived(gpeer, gate_s.at[0], gate_r.at[0])
     lax.fori_loop(0, NG, project, 0)
 
     for way in range(2):
@@ -639,6 +651,7 @@
         pltpu.VMEM((64, CH), BF16),
         pltpu.VMEM((64, CH), BF16),
         pltpu.VMEM((64, CH), BF16),
+        pltpu.VMEM((NG, 2, 64, W), F32),
         pltpu.VMEM((NZ, NG, 16, W), BF16),
         pltpu.VMEM((2, 2, 16, W), BF16),
         pltpu.VMEM((2, 3, NG, 16, W), BF16),

time: 110 us -> 110 us (level)
  no operation moved by 1% of the time
where the time goes in v4:
time: 110 us; the launch traced here: 109 us
  Pallas kernels  108 us (98%)
  local copies, waits for them, and re-layouts  1.47 us (1%)
    pallas_call x1, Pallas kernels, per_device(): pl.pallas_call(layer_kernel, out_shape=jax.ShapeDtypeStruct(residual.shap...  108 us

profile of v4, /device:TPU:1, one launch (start us, length us, event | category | flops | bytes accessed | tf_op | source)
XLA Modules:
  0.0 109.4 jit_solution(13965513235578773447)
XLA Ops:
  0.0 107.9 %shard_map.136 = bf16[8,4096]{1,0:T(8,128)(2,1)} custom-call(bf16[8,4096]{1,0:T(8,128)(2,1)} %residual_hbm.1, bf16[128,512]{1,0:T(8,128)(2,1)} %xin_hbm.1, bf16[128,512]{1,0:T(8,128)(2,1)} %gate_hbm.1, f32[128,512]{1,0:T(8,128)} %step_hbm.1, f32[16,512]{1,0:T(8,128)} %rate_hbm.1, f32[16,128]{1,0:T(8,128)} %bitcast.7, f32[16,128]{1,0:T(8,128)} %bitcast.8, ...), custom_call_target="tpu_custom_call" | custom-call | tf_op jit(solution)/shard_map/pallas_call | solution.py:708
  107.9 1.5 %copy.16 = bf16[8,4096]{1,0:T(8,128)(2,1)} copy(bf16[8,4096]{1,0:T(8,128)(2,1)} %shard_map.136) | data formatting | bytes 131072
